TPU v7x, 32 devices: a whole 2x2x4 slice. The times are simulated.
32 devices in a mesh: axial: 8 (over y, x, core), pitch: 4 (over z).
Axes of the slice: x: 2, y: 2, z: 4, core: 2. Of those that a mesh axis runs over, the one named last changes fastest.
Arguments:
- fluid_temp: float32 [512, 256, 128], P('axial', 'pitch'), may hold values from -6 to 6
- axial_speed: float32 [512, 256, 128], P('axial', 'pitch'), may hold values from 0.05 to 0.4
- pitch_speed: float32 [512, 256, 128], P('axial', 'pitch'), may hold values from -0.25 to 0.25
- fourier_store: float32 [2, 512, 128], P(None, 'axial'), may hold values from -6 to 6
- wall_temp: float32 [32768, 128], P(('axial', 'pitch')), may hold values from -6 to 6
- wall_cell: int32 [32768], P(('axial', 'pitch')), may hold values from 0 to 4095
- wall_owner: int32 [32768, 1], P(('axial', 'pitch')), may hold values from 0 to 31; in each aligned block of 1024 rows (0 to 1023, 1024 to 2047, ...) at most 64 rows name the same one
- wall_target: int32 [32768], P(('axial', 'pitch')), may hold values from 0 to 127
- wall_count: int32 [32], P(('axial', 'pitch')), may hold values from 1 to 1024, 24576 in all
- metal_temp: float32 [512, 48, 512], P('axial', None, 'pitch'), may hold values from -6 to 6
- metal_diag: float32 [512, 48, 512], P('axial', None, 'pitch'), may hold values from 0.5 to 2
Outputs:
- fluid_out: float32 [512, 256, 128], P('axial', 'pitch')
- metal_out: float32 [512, 48, 512], P('axial', None, 'pitch')
- wall_update: float32 [32768, 128], P(('axial', 'pitch'))
Inputs may be any that keep to these rules, and one draw needn't show every extreme that they name: `wall_owner`: within the rows of one device no owner appears more than 64 times, and some owner appears exactly 64 times. `wall_count`: some device has all 1024 rows live.
All inputs are finite; a program needn't handle non-finite values.
Results may differ from a plain program's by a relative error of at most 0.0003.
Values sent between devices are 32-bit elements; how exact they have to be, the bound alone decides.
A program may use at most 192 MiB of HBM per device.

v0:
```python
import functools

import jax
import jax.numpy as jnp
from jax import lax
from jax.experimental import pallas as pl
from jax.experimental.pallas import tpu as pltpu
from jax.sharding import PartitionSpec as P

SWEEPS = 4
KAPPA = 0.1
HEAT = 0.3
PHASE_COS = 0.8
PHASE_SIN = 0.6
LOW_BOUND = 0.5
HIGH_BOUND = 14.0
THETA = 0.5 * (HIGH_BOUND + LOW_BOUND)
DELTA = 0.5 * (HIGH_BOUND - LOW_BOUND)
MESH = pl.DeviceIdType.MESH
F32 = jnp.float32
BF16 = jnp.bfloat16


def cheb_factors():
    ratio = THETA / DELTA
    rho = 1.0 / ratio
    factors = []
    for _ in range(SWEEPS - 1):
        rho_new = 1.0 / (2.0 * ratio - rho)
        factors.append((rho_new * rho, 2.0 * rho_new / DELTA))
        rho = rho_new
    return factors


def two_parts(value):
    hi = value.astype(BF16)
    lo = (value - hi.astype(F32)).astype(BF16)
    return hi, lo


def kernel(
    na, npi, cap,
    cell_s, key_s, count_s,
    cell_v, key_v, ids_v, wall, fourier, aspeed, pspeed, diag, fluid_hbm, metal_hbm,
    fluid_out, metal_out, wall_out,
    upad, spad, avg, wsum, wcnt, face, ph, wcat, rows, fcat,
    xpad, da, db, res, mh, mpack, inj,
    snd, rcv, bsnd, brcv,
    lsem, fsend, frecv, msend, mrecv, asend, arecv,
):
    ax = lax.axis_index("axial")
    pz = lax.axis_index("pitch")
    devices = na * npi
    me = ax * npi + pz
    ca, cp, nr = aspeed.shape
    mc, mt, _ = diag.shape
    slots = wall.shape[0]
    group = nr // cap

    def dev(e):
        return (lax.div(e, npi), lax.rem(e, npi))

    up_axial = (jnp.minimum(ax + 1, na - 1), pz)
    dn_axial = (jnp.maximum(ax - 1, 0), pz)
    north_dev = (ax, lax.rem(pz + 1, npi))
    south_dev = (ax, lax.rem(pz + npi - 1, npi))
    has_dn, has_up = ax > 0, ax < na - 1
    has_lo, has_hi = pz > 0, pz < npi - 1

    ucopy = pltpu.make_async_copy(fluid_hbm, upad.at[pl.ds(1, ca)], lsem.at[0])
    xcopy = pltpu.make_async_copy(metal_hbm, xpad.at[pl.ds(1, mc)], lsem.at[1])
    ucopy.start()
    xcopy.start()

    barrier = pltpu.get_barrier_semaphore()

    @pl.loop(1, devices)
    def _(o):
        pl.semaphore_signal(
            barrier, inc=1, device_id=dev(lax.rem(me + o, devices)), device_id_type=MESH
        )

    def remote(src, dst, ssem, rsem, device):
        return pltpu.make_async_remote_copy(
            src_ref=src, dst_ref=dst, send_sem=ssem, recv_sem=rsem,
            device_id=device, device_id_type=MESH,
        )

    def fluid_copies(pad, st):
        return (
            (has_up, has_dn, remote(pad.at[ca], pad.at[0], fsend.at[st, 0], frecv.at[st, 0], up_axial)),
            (has_dn, has_up, remote(pad.at[1], pad.at[ca + 1], fsend.at[st, 1], frecv.at[st, 1], dn_axial)),
            (None, None, remote(face.at[st, 1], ph.at[st, 0], fsend.at[st, 2], frecv.at[st, 2], north_dev)),
            (None, None, remote(face.at[st, 0], ph.at[st, 1], fsend.at[st, 3], frecv.at[st, 3], south_dev)),
        )

    def metal_copies(pad, st):
        return (
            (has_up, has_dn, remote(pad.at[mc], mh.at[st, 0], msend.at[st, 0], mrecv.at[st, 0], up_axial)),
            (has_dn, has_up, remote(pad.at[1], mh.at[st, 1], msend.at[st, 1], mrecv.at[st, 1], dn_axial)),
            (has_hi, has_lo, remote(mpack.at[st], mh.at[st, 2], msend.at[st, 2], mrecv.at[st, 2], north_dev)),
            (has_lo, has_hi, remote(mpack.at[st], mh.at[st, 3], msend.at[st, 3], mrecv.at[st, 3], south_dev)),
        )

    def when(condition, action):
        if condition is None:
            action()
        else:
            pl.when(condition)(action)

    def start(copies):
        for sends, _, copy in copies:
            when(sends, copy.start)

    def wait_sent(copies):
        for sends, _, copy in copies:
            when(sends, copy.wait_send)

    def wait_got(copies):
        for _, gets, copy in copies:
            when(gets, copy.wait_recv)

    lane_m = lax.broadcasted_iota(jnp.int32, (mt, nr), 1)
    row_m = lax.broadcasted_iota(jnp.int32, (mt, nr), 0)
    lane_f = lax.broadcasted_iota(jnp.int32, (cp, nr), 1)
    row_f = lax.broadcasted_iota(jnp.int32, (cp, nr), 0)

    def pack_in(acc, tile, c):
        return jnp.where(lax.div(lane_m, 2) == c, pltpu.roll(tile, 2 * c + 1, 1), acc)

    def pack(pad):
        return lax.fori_loop(
            0, mc, lambda c, acc: pack_in(acc, pad[c + 1], c), jnp.zeros((mt, nr), F32), unroll=2
        )

    wall_rows = wall[...]
    w_hi, w_lo = two_parts(wall_rows)
    wcat[:, 0:nr] = w_hi
    wcat[:, nr:2 * nr] = w_lo
    wcat[:, 2 * nr:3 * nr] = jnp.ones((slots, nr), BF16)

    ucopy.wait()
    xcopy.wait()

    @pl.loop(0, ca)
    def _(a):
        face[0, 0, pl.ds(a, 1), :] = upad[a + 1, 0:1, :]
        face[0, 1, pl.ds(a, 1), :] = upad[a + 1, cp - 1:cp, :]

    mpack[0] = pack(xpad)

    pl.semaphore_wait(barrier, devices - 1)
    first = fluid_copies(upad, 0)
    start(first)
    mcopy = [metal_copies(pad, st) for st, pad in enumerate((xpad, da, db))]
    mcopy.append(metal_copies(da, 3))
    start(mcopy[0])

    chunk = min(512, ca * cp)

    @pl.loop(0, ca * cp // chunk)
    def _(i):
        at = lax.broadcasted_iota(jnp.int32, (chunk, slots), 0) + i * chunk
        hot = jnp.where(at == cell_v[...], 1.0, 0.0).astype(BF16)
        sums = jnp.dot(hot, wcat[...], preferred_element_type=F32)
        base = pl.multiple_of(i * chunk, chunk)
        wsum[pl.ds(base, chunk), :] = sums[:, 0:nr] + sums[:, nr:2 * nr]
        wcnt[pl.ds(base, chunk), :] = sums[:, 2 * nr:3 * nr]

    def edges(pad, st):
        wait_got(fluid_copies(pad, st))

        @pl.when(ax == 0)
        def _():
            pad[0] = pad[1]

        @pl.when(ax == na - 1)
        def _():
            pad[ca + 1] = pad[ca]

        @pl.when(pz == 0)
        def _():
            ph[st, 0] = PHASE_COS * ph[st, 0] + PHASE_SIN * fourier[0]

        @pl.when(pz == npi - 1)
        def _():
            ph[st, 1] = PHASE_COS * ph[st, 1] + PHASE_SIN * fourier[1]

    def rate(pad, st, a):
        temp = pad[a + 1]
        east, west = pad[a + 2], pad[a]
        north = jnp.where(row_f == cp - 1, ph[st, 1, pl.ds(a, 1), :], pltpu.roll(temp, cp - 1, 0))
        south = jnp.where(row_f == 0, ph[st, 0, pl.ds(a, 1), :], pltpu.roll(temp, 1, 0))
        outer = jnp.where(lane_f == nr - 1, temp, pltpu.roll(temp, nr - 1, 1))
        inner = jnp.where(lane_f == 0, temp, pltpu.roll(temp, 1, 1))
        spread = east + west + north + south + outer + inner - 6.0 * temp
        base = pl.multiple_of(a * cp, cp)
        sink = HEAT * (wcnt[pl.ds(base, cp), :] * temp - wsum[pl.ds(base, cp), :])
        return temp, (
            -0.5 * aspeed[a] * (east - west) - 0.5 * pspeed[a] * (north - south) + KAPPA * spread - sink
        )

    edges(upad, 0)

    @pl.loop(0, ca)
    def _(a):
        temp, change = rate(upad, 0, a)
        section = temp + change
        spad[a + 1] = section
        avg[pl.ds(pl.multiple_of(a * cp, cp), cp), :] = 0.5 * (temp + section)
        face[1, 0, pl.ds(a, 1), :] = section[0:1]
        face[1, 1, pl.ds(a, 1), :] = section[cp - 1:cp]

    second = fluid_copies(spad, 1)
    start(second)

    @pl.loop(0, slots // 16)
    def _(i):
        for j in range(16):
            s = i * 16 + j
            rows[pl.ds(s, 1), :] = avg[pl.ds(cell_s[s], 1), :]

    f_hi, f_lo = two_parts(HEAT * (rows[...] - wall[...]))
    fcat[:, 0:nr] = f_hi
    fcat[:, nr:2 * nr] = f_lo

    send_chunk = min(512, devices * cap)
    owners = send_chunk // cap

    @pl.loop(0, devices * cap // send_chunk)
    def _(i):
        at = lax.broadcasted_iota(jnp.int32, (send_chunk, slots), 0) + i * send_chunk
        hot = jnp.where(at == key_v[...], 1.0, 0.0).astype(BF16)
        sums = jnp.dot(hot, fcat[...], preferred_element_type=F32)
        part = (sums[:, 0:nr] + sums[:, nr:2 * nr]).reshape(owners, cap, nr)
        snd[pl.ds(i * owners, owners), 0:cap, :] = part
        snd[pl.ds(i * owners, owners), cap:cap + 8, :] = ids_v[pl.ds(i * owners, owners)]

    def out_copy(o):
        e = lax.rem(me + o, devices)
        return remote(snd.at[e], rcv.at[me], asend.at[0, o], arecv.at[0, o], dev(e))

    def in_copy(o):
        e = lax.rem(me - o + devices, devices)
        return remote(snd.at[e], rcv.at[e], asend.at[0, o], arecv.at[0, o], dev(e))

    @pl.loop(1, devices)
    def _(o):
        out_copy(o).start()

    rcv[me] = snd[me]

    def spans(st):
        wait_got(mcopy[st])
        lower = jnp.where(has_lo, pltpu.roll(mh[st, 2], 1, 1), 0.0)
        upper = jnp.where(has_hi, pltpu.roll(mh[st, 3], nr - 1, 1), 0.0)
        return jnp.where(lax.rem(lane_m, 2) == 0, upper, lower)

    def ends(pad, st):
        @pl.when(has_dn)
        def _():
            pad[0] = mh[st, 0]

        @pl.when(has_up)
        def _():
            pad[mc + 1] = mh[st, 1]

    def beside(pad, comb, c):
        tile = pad[c + 1]
        edge = pltpu.roll(comb, nr - 1 - 2 * c, 1)
        total = pad[c] + pad[c + 2]
        total = total + jnp.where(row_m == 0, 0.0, pltpu.roll(tile, 1, 0))
        total = total + jnp.where(row_m == mt - 1, 0.0, pltpu.roll(tile, mt - 1, 0))
        total = total + jnp.where(lane_m == 0, edge, pltpu.roll(tile, 1, 1))
        return tile, total + jnp.where(lane_m == nr - 1, edge, pltpu.roll(tile, nr - 1, 1))

    zero = jnp.zeros((mt, nr), F32)
    for pad in (xpad, da, db):
        pad[0] = zero
        pad[mc + 1] = zero

    comb = spans(0)
    ends(xpad, 0)

    @pl.loop(0, mc)
    def _(c):
        tile, around = beside(xpad, comb, c)
        start_res = around - 6.0 * tile
        res[c] = start_res
        da[c + 1] = start_res * (1.0 / THETA)

    edges(spad, 1)

    @pl.loop(0, ca)
    def _(a):
        temp, change = rate(spad, 1, a)
        fluid_out[a] = avg[pl.ds(pl.multiple_of(a * cp, cp), cp), :] + 0.5 * change

    @pl.loop(1, devices)
    def _(o):
        in_copy(o).wait_recv()

    lane_p = lax.broadcasted_iota(jnp.int32, (8, nr), 1)
    row_p = lax.broadcasted_iota(jnp.int32, (2 * mc, nr), 0).astype(F32) + 1.0

    def place(g):
        ids = rcv[g * group, cap:cap + 8, :]
        for j in range(1, group):
            ids = jnp.where(lax.div(lane_p, cap) == j, rcv[g * group + j, cap:cap + 8, :], ids)
        return jnp.where(row_p == ids[0:1], 1.0, 0.0)

    def gather_in(g, total):
        part = rcv[pl.ds(g * group, group), 0:cap, :].reshape(nr, nr)
        p_hi, p_lo = two_parts(part)
        hot = place(g).astype(BF16)
        return total + (
            jnp.dot(hot, p_hi, preferred_element_type=F32)
            + jnp.dot(hot, p_lo, preferred_element_type=F32)
        )

    inj[...] = lax.fori_loop(0, devices // group, gather_in, jnp.zeros((2 * mc, nr), F32), unroll=4)

    row_e = lax.broadcasted_iota(jnp.int32, (8, nr), 0)

    @pl.loop(0, mc)
    def _(c):
        low = jnp.where(row_e == 0, inj[pl.ds(2 * c, 1), :], 0.0)
        high = jnp.where(row_e == 7, inj[pl.ds(2 * c + 1, 1), :], 0.0)
        res[c, 0:8, :] = res[c, 0:8, :] + low
        res[c, mt - 8:mt, :] = res[c, mt - 8:mt, :] + high
        da[c + 1, 0:8, :] = da[c + 1, 0:8, :] + low * (1.0 / THETA)
        da[c + 1, mt - 8:mt, :] = da[c + 1, mt - 8:mt, :] + high * (1.0 / THETA)

    mpack[1] = pack(da)
    start(mcopy[1])

    factors = cheb_factors()
    for sweep, (old, new) in enumerate(((da, db), (db, da))):
        st = sweep + 1
        comb = spans(st)
        ends(old, st)
        if sweep == 1:
            wait_sent(mcopy[1])
        f0, f1 = factors[sweep]

        def step(c, acc, old=old, new=new, comb=comb, f0=f0, f1=f1, sweep=sweep):
            tile, around = beside(old, comb, c)
            base = xpad[c + 1] if sweep == 0 else metal_out[c]
            metal_out[c] = base + tile
            left = res[c] - ((6.0 + diag[c]) * tile - around)
            res[c] = left
            fresh = f0 * tile + f1 * left
            new[c + 1] = fresh
            return pack_in(acc, fresh, c)

        mpack[st + 1] = lax.fori_loop(0, mc, step, jnp.zeros((mt, nr), F32))
        start(mcopy[st + 1])

    comb = spans(3)
    ends(da, 3)
    f0, f1 = factors[2]

    @pl.loop(0, mc)
    def _(c):
        tile, around = beside(da, comb, c)
        left = res[c] - ((6.0 + diag[c]) * tile - around)
        done = metal_out[c] + tile + (f0 * tile + f1 * left)
        metal_out[c] = done
        inj[pl.ds(2 * c, 1), :] = done[0:1]
        inj[pl.ds(2 * c + 1, 1), :] = done[mt - 1:mt]

    b_hi, b_lo = two_parts(inj[...])
    bcat = jnp.concatenate([b_hi, b_lo], axis=1)

    @pl.loop(0, devices // group)
    def _(g):
        hot = place(g).T.astype(BF16)
        sums = jnp.dot(hot, bcat, preferred_element_type=F32)
        bsnd[pl.ds(pl.multiple_of(g * nr, nr), nr), :] = sums[:, 0:nr] + sums[:, nr:2 * nr]

    def block(ref, e):
        return ref.at[pl.ds(pl.multiple_of(e * cap, cap), cap)]

    def back_out(o):
        e = lax.rem(me + o, devices)
        return remote(block(bsnd, e), block(brcv, me), asend.at[1, o], arecv.at[1, o], dev(e))

    def back_in(o):
        e = lax.rem(me - o + devices, devices)
        return remote(block(bsnd, e), block(brcv, e), asend.at[1, o], arecv.at[1, o], dev(e))

    @pl.loop(1, devices)
    def _(o):
        back_out(o).start()

    own = pl.ds(pl.multiple_of(me * cap, cap), cap)
    brcv[own, :] = bsnd[own, :]

    wait_sent(first)
    wait_sent(second)
    wait_sent(mcopy[0])
    wait_sent(mcopy[2])
    wait_sent(mcopy[3])

    @pl.loop(1, devices)
    def _(o):
        out_copy(o).wait_send()

    @pl.loop(1, devices)
    def _(o):
        back_in(o).wait_recv()

    @pl.loop(0, slots // 16)
    def _(i):
        for j in range(16):
            s = i * 16 + j
            rows[pl.ds(s, 1), :] = brcv[pl.ds(key_s[s], 1), :]

    live = lax.broadcasted_iota(jnp.int32, (slots, nr), 0) < count_s[0]
    wall_out[...] = jnp.where(live, 0.5 * (wall[...] + rows[...]), wall[...])

    @pl.loop(1, devices)
    def _(o):
        back_out(o).wait_send()


def on_device(
    na, npi,
    fluid_temp, axial_speed, pitch_speed, fourier_store, wall_temp, wall_cell,
    wall_owner, wall_target, wall_count, metal_temp, metal_diag,
):
    devices = na * npi
    slots = wall_temp.shape[0]
    ca, cp, nr = fluid_temp.shape
    mc, mt, _ = metal_temp.shape
    cap = max(2, 2 * slots // devices)
    order = jnp.arange(slots, dtype=jnp.int32)
    live = order < wall_count[0]
    owner = wall_owner[:, 0]
    earlier = (owner[:, None] == owner[None, :]) & live[None, :] & (order[None, :] < order[:, None])
    rank = jnp.sum(earlier.astype(jnp.int32), axis=1)
    key = jnp.where(live, owner * cap + rank, -1)
    spots = jnp.arange(devices * cap, dtype=jnp.int32)
    ids = jnp.sum(
        jnp.where(spots[:, None] == key[None, :], (wall_target + 1).astype(F32)[None, :], 0.0), axis=1
    ).reshape(devices, 1, 1, cap)
    ids = jnp.broadcast_to(ids, (devices, 8, nr // cap, cap)).reshape(devices, 8, nr)
    cell_row = jnp.where(live, wall_cell, -1)[None, :]
    vmem = pl.BlockSpec(memory_space=pltpu.VMEM)
    smem = pl.BlockSpec(memory_space=pltpu.SMEM)
    hbm = pl.BlockSpec(memory_space=pl.ANY)
    dma = pltpu.SemaphoreType.DMA
    return pl.pallas_call(
        functools.partial(kernel, na, npi, cap),
        out_shape=(
            jax.ShapeDtypeStruct((ca, cp, nr), F32),
            jax.ShapeDtypeStruct((mc, mt, nr), F32),
            jax.ShapeDtypeStruct((slots, nr), F32),
        ),
        in_specs=[smem] * 3 + [vmem] * 8 + [hbm] * 2,
        out_specs=(vmem, vmem, vmem),
        scratch_shapes=[
            pltpu.VMEM((ca + 2, cp, nr), F32),
            pltpu.VMEM((ca + 2, cp, nr), F32),
            pltpu.VMEM((ca * cp, nr), F32),
            pltpu.VMEM((ca * cp, nr), F32),
            pltpu.VMEM((ca * cp, nr), F32),
            pltpu.VMEM((2, 2, ca, nr), F32),
            pltpu.VMEM((2, 2, ca, nr), F32),
            pltpu.VMEM((slots, 3 * nr), BF16),
            pltpu.VMEM((slots, nr), F32),
            pltpu.VMEM((slots, 2 * nr), BF16),
            pltpu.VMEM((mc + 2, mt, nr), F32),
            pltpu.VMEM((mc + 2, mt, nr), F32),
            pltpu.VMEM((mc + 2, mt, nr), F32),
            pltpu.VMEM((mc, mt, nr), F32),
            pltpu.VMEM((4, 4, mt, nr), F32),
            pltpu.VMEM((4, mt, nr), F32),
            pltpu.VMEM((2 * mc, nr), F32),
            pltpu.VMEM((devices, cap + 8, nr), F32),
            pltpu.VMEM((devices, cap + 8, nr), F32),
            pltpu.VMEM((devices * cap, nr), F32),
            pltpu.VMEM((devices * cap, nr), F32),
            dma((2,)),
            dma((2, 4)),
            dma((2, 4)),
            dma((4, 4)),
            dma((4, 4)),
            dma((2, devices)),
            dma((2, devices)),
        ],
        compiler_params=pltpu.CompilerParams(
            collective_id=0, has_side_effects=True, vmem_limit_bytes=56 * 1024 * 1024
        ),
        name="window",
    )(
        wall_cell, jnp.maximum(key, 0), wall_count,
        cell_row, key[None, :], ids, wall_temp, fourier_store, axial_speed, pitch_speed,
        metal_diag, fluid_temp, metal_temp,
    )


def solution(mesh):
    placed = (
        P("axial", "pitch", None),
        P("axial", "pitch", None),
        P("axial", "pitch", None),
        P(None, "axial", None),
        P(("axial", "pitch"), None),
        P(("axial", "pitch")),
        P(("axial", "pitch"), None),
        P(("axial", "pitch")),
        P(("axial", "pitch")),
        P("axial", None, "pitch"),
        P("axial", None, "pitch"),
    )
    return jax.shard_map(
        functools.partial(on_device, mesh.shape["axial"], mesh.shape["pitch"]),
        mesh=mesh,
        in_specs=placed,
        out_specs=(
            P("axial", "pitch", None),
            P("axial", None, "pitch"),
            P(("axial", "pitch"), None),
        ),
        check_vma=False,
    )
```

profile of v0, /device:TPU:0, one launch (start us, length us, event | category | flops | bytes accessed | tf_op | source)
XLA Modules:
  0.0 138.5 jit_solution(5438427286590379434)
XLA Ops:
  1.3 1.4 convert_reduce_fusion
  2.7 1.3 compare_select_fusion.key_v
  4.0 0.7 add_convert_fusion
  4.6 1.3 broadcast_maximum_fusion
  6.0 0.9 select_reduce_fusion
  6.9 0.1 broadcast_in_dim.45
  7.0 0.1 broadcast_in_dim.47
  7.1 0.7 broadcast_in_dim.48.ids_v
  7.7 125.3 %window.1 = (f32[64,64,128]{2,1,0:T(8,128)}, f32[64,48,128]{2,1,0:T(8,128)}, f32[1024,128]{1,0:T(8,128)}) custom-call(s32[1024]{0:T(1024)} %cell_s.1, s32[1024]{0:T(1024)} %get-tuple-element.3.key_s, s32[1]{0:T(128)} %copy.17.count_s, s32[1,1024]{1,0:T(1,128)} %bitcast.11, s32[1,1024]{1,0:T(1,128)} %compare_select_fusion.key_v, ...), custom_call_target="tpu_custom_call" | custom-call | tf_op jit(solution)/shard_map/window/pallas_call | solution.py:453
  133.0 0.0 copy-start
  133.0 3.3 %copy.18 = f32[64,64,128]{2,1,0:T(8,128)} copy(f32[64,64,128]{2,1,0:T(8,128)} %get-tuple-element.9) | data formatting | bytes 4194304
  136.3 0.0 copy-done
  136.3 0.0 copy-start.1
  136.3 1.1 copy.19
  137.4 0.3 copy-done.1
  137.7 0.8 copy.20
  (2 shorter events, 0.0 us)
Async XLA Ops:
  133.0 3.3 %copy-start = (f32[64,48,128]{2,1,0:T(8,128)S(1)}, f32[64,48,128]{2,1,0:T(8,128)}, u32[]{:S(2)}) copy-start(f32[64,48,128]{2,1,0:T(8,128)} %get-tuple-element.10) | copy-start | bytes 4718596
  136.3 1.4 %copy-start.1 = (f32[1024,128]{1,0:T(8,128)S(1)}, f32[1024,128]{1,0:T(8,128)}, u32[]{:S(2)}) copy-start(f32[1024,128]{1,0:T(8,128)} %get-tuple-element.11) | copy-start | bytes 1572868
where the time goes:
time: 139 us; the launch traced here: 138 us
  Pallas kernels  125 us (90%)
  local copies, waits for them, and re-layouts  6.31 us (5%)
  other arithmetic  5.58 us (4%)
    pallas_call x1, Pallas kernels, on_device(): pl.pallas_call(functools.partial(kernel, na, npi, cap), out_shape=(jax.Sh...  125 us
    unnamed x7, local copies, waits for them, and re-layouts  5.47 us

commit v1 on v0

--- a/solution.py
+++ b/solution.py
@@ -45,20 +45,16 @@
     fluid_out, metal_out, wall_out,
     upad, spad, avg, wsum, wcnt, face, ph, wcat, rows, fcat,
     xpad, da, db, res, mh, mpack, inj,
-    snd, rcv, bsnd, brcv,
-    lsem, fsend, frecv, msend, mrecv, asend, arecv,
+    snd, rcv, bsnd, brcv, part_snd, part_rcv, bound,
+    lsem, fsend, frecv, msend, mrecv, asend, arecv, psend, precv,
 ):
     ax = lax.axis_index("axial")
     pz = lax.axis_index("pitch")
     devices = na * npi
-    me = ax * npi + pz
     ca, cp, nr = aspeed.shape
     mc, mt, _ = diag.shape
     slots = wall.shape[0]
     group = nr // cap
-
-    def dev(e):
-        return (lax.div(e, npi), lax.rem(e, npi))
 
     up_axial = (jnp.minimum(ax + 1, na - 1), pz)
     dn_axial = (jnp.maximum(ax - 1, 0), pz)
@@ -74,11 +70,16 @@
 
     barrier = pltpu.get_barrier_semaphore()
 
-    @pl.loop(1, devices)
-    def _(o):
-        pl.semaphore_signal(
-            barrier, inc=1, device_id=dev(lax.rem(me + o, devices)), device_id_type=MESH
-        )
+    def axial_peer(o):
+        return lax.rem(ax + o, na)
+
+    def pitch_peer(o):
+        return lax.rem(pz + o, npi)
+
+    for o in range(1, na):
+        pl.semaphore_signal(barrier, inc=1, device_id=(axial_peer(o), pz), device_id_type=MESH)
+    for o in range(1, npi):
+        pl.semaphore_signal(barrier, inc=1, device_id=(ax, pitch_peer(o)), device_id_type=MESH)
 
     def remote(src, dst, ssem, rsem, device):
         return pltpu.make_async_remote_copy(
@@ -130,7 +131,7 @@
 
     def pack(pad):
         return lax.fori_loop(
-            0, mc, lambda c, acc: pack_in(acc, pad[c + 1], c), jnp.zeros((mt, nr), F32), unroll=2
+            0, mc, lambda c, acc: pack_in(acc, pad[c + 1], c), jnp.zeros((mt, nr), F32), unroll=8
         )
 
     wall_rows = wall[...]
@@ -142,14 +143,14 @@
     ucopy.wait()
     xcopy.wait()
 
-    @pl.loop(0, ca)
+    @pl.loop(0, ca, unroll=2)
     def _(a):
         face[0, 0, pl.ds(a, 1), :] = upad[a + 1, 0:1, :]
         face[0, 1, pl.ds(a, 1), :] = upad[a + 1, cp - 1:cp, :]
 
     mpack[0] = pack(xpad)
 
-    pl.semaphore_wait(barrier, devices - 1)
+    pl.semaphore_wait(barrier, na + npi - 2)
     first = fluid_copies(upad, 0)
     start(first)
     mcopy = [metal_copies(pad, st) for st, pad in enumerate((xpad, da, db))]
@@ -202,7 +203,7 @@
 
     edges(upad, 0)
 
-    @pl.loop(0, ca)
+    @pl.loop(0, ca, unroll=2)
     def _(a):
         temp, change = rate(upad, 0, a)
         section = temp + change
@@ -236,19 +237,23 @@
         snd[pl.ds(i * owners, owners), 0:cap, :] = part
         snd[pl.ds(i * owners, owners), cap:cap + 8, :] = ids_v[pl.ds(i * owners, owners)]
 
-    def out_copy(o):
-        e = lax.rem(me + o, devices)
-        return remote(snd.at[e], rcv.at[me], asend.at[0, o], arecv.at[0, o], dev(e))
+    def out_copy(o, j):
+        return remote(
+            snd.at[pl.ds(j * npi, npi)], rcv.at[pl.ds(ax * npi, npi)], asend.at[0, o], arecv.at[0, o],
+            (axial_peer(o), pz),
+        )
 
     def in_copy(o):
-        e = lax.rem(me - o + devices, devices)
-        return remote(snd.at[e], rcv.at[e], asend.at[0, o], arecv.at[0, o], dev(e))
-
-    @pl.loop(1, devices)
-    def _(o):
-        out_copy(o).start()
-
-    rcv[me] = snd[me]
+        i = lax.rem(ax - o + na, na)
+        return remote(
+            snd.at[pl.ds(i * npi, npi)], rcv.at[pl.ds(i * npi, npi)], asend.at[0, o], arecv.at[0, o],
+            (i, pz),
+        )
+
+    for o in range(1, na):
+        out_copy(o, axial_peer(o)).start()
+
+    rcv[pl.ds(ax * npi, npi)] = snd[pl.ds(ax * npi, npi)]
 
     def spans(st):
         wait_got(mcopy[st])
@@ -282,7 +287,7 @@
     comb = spans(0)
     ends(xpad, 0)
 
-    @pl.loop(0, mc)
+    @pl.loop(0, mc, unroll=4)
     def _(c):
         tile, around = beside(xpad, comb, c)
         start_res = around - 6.0 * tile
@@ -291,38 +296,61 @@
 
     edges(spad, 1)
 
-    @pl.loop(0, ca)
+    @pl.loop(0, ca, unroll=2)
     def _(a):
         temp, change = rate(spad, 1, a)
         fluid_out[a] = avg[pl.ds(pl.multiple_of(a * cp, cp), cp), :] + 0.5 * change
 
-    @pl.loop(1, devices)
-    def _(o):
+    for o in range(1, na):
         in_copy(o).wait_recv()
 
     lane_p = lax.broadcasted_iota(jnp.int32, (8, nr), 1)
     row_p = lax.broadcasted_iota(jnp.int32, (2 * mc, nr), 0).astype(F32) + 1.0
-
-    def place(g):
-        ids = rcv[g * group, cap:cap + 8, :]
-        for j in range(1, group):
-            ids = jnp.where(lax.div(lane_p, cap) == j, rcv[g * group + j, cap:cap + 8, :], ids)
-        return jnp.where(row_p == ids[0:1], 1.0, 0.0)
-
-    def gather_in(g, total):
-        part = rcv[pl.ds(g * group, group), 0:cap, :].reshape(nr, nr)
-        p_hi, p_lo = two_parts(part)
-        hot = place(g).astype(BF16)
-        return total + (
-            jnp.dot(hot, p_hi, preferred_element_type=F32)
-            + jnp.dot(hot, p_lo, preferred_element_type=F32)
-        )
-
-    inj[...] = lax.fori_loop(0, devices // group, gather_in, jnp.zeros((2 * mc, nr), F32), unroll=4)
+    span = min(group, na)
+    width = span * cap
+
+    def place(g, z):
+        ids = rcv[g * span * npi + z, cap:cap + 8, :]
+        for j in range(1, span):
+            ids = jnp.where(
+                lax.div(lane_p, cap) == j, rcv[(g * span + j) * npi + z, cap:cap + 8, :], ids
+            )
+        return jnp.where(row_p[:, 0:width] == ids[0:1, 0:width], 1.0, 0.0)
+
+    def injected(z):
+        def gather_in(g, total):
+            part = jnp.concatenate(
+                [rcv[(g * span + j) * npi + z, 0:cap, :] for j in range(span)], axis=0
+            )
+            p_hi, p_lo = two_parts(part)
+            hot = place(g, z).astype(BF16)
+            return total + (
+                jnp.dot(hot, p_hi, preferred_element_type=F32)
+                + jnp.dot(hot, p_lo, preferred_element_type=F32)
+            )
+
+        total = jnp.zeros((2 * mc, nr), F32)
+        for g in range(na // span):
+            total = gather_in(g, total)
+        return total
+
+    def part_out(o):
+        return remote(
+            part_snd.at[o], part_rcv.at[o], psend.at[0, o], precv.at[0, o], (ax, pitch_peer(o))
+        )
+
+    for o in range(1, npi):
+        part_snd[o] = injected(pitch_peer(o))
+        part_out(o).start()
+    mine = injected(pz)
+    for o in range(1, npi):
+        part_out(o).wait_recv()
+        mine = mine + part_rcv[o]
+    inj[...] = mine
 
     row_e = lax.broadcasted_iota(jnp.int32, (8, nr), 0)
 
-    @pl.loop(0, mc)
+    @pl.loop(0, mc, unroll=4)
     def _(c):
         low = jnp.where(row_e == 0, inj[pl.ds(2 * c, 1), :], 0.0)
         high = jnp.where(row_e == 7, inj[pl.ds(2 * c + 1, 1), :], 0.0)
@@ -353,14 +381,14 @@
             new[c + 1] = fresh
             return pack_in(acc, fresh, c)
 
-        mpack[st + 1] = lax.fori_loop(0, mc, step, jnp.zeros((mt, nr), F32))
+        mpack[st + 1] = lax.fori_loop(0, mc, step, jnp.zeros((mt, nr), F32), unroll=4)
         start(mcopy[st + 1])
 
     comb = spans(3)
     ends(da, 3)
     f0, f1 = factors[2]
 
-    @pl.loop(0, mc)
+    @pl.loop(0, mc, unroll=4)
     def _(c):
         tile, around = beside(da, comb, c)
         left = res[c] - ((6.0 + diag[c]) * tile - around)
@@ -369,31 +397,47 @@
         inj[pl.ds(2 * c, 1), :] = done[0:1]
         inj[pl.ds(2 * c + 1, 1), :] = done[mt - 1:mt]
 
-    b_hi, b_lo = two_parts(inj[...])
-    bcat = jnp.concatenate([b_hi, b_lo], axis=1)
-
-    @pl.loop(0, devices // group)
-    def _(g):
-        hot = place(g).T.astype(BF16)
-        sums = jnp.dot(hot, bcat, preferred_element_type=F32)
-        bsnd[pl.ds(pl.multiple_of(g * nr, nr), nr), :] = sums[:, 0:nr] + sums[:, nr:2 * nr]
-
-    def block(ref, e):
-        return ref.at[pl.ds(pl.multiple_of(e * cap, cap), cap)]
+    bound[0] = inj[...]
+
+    def bound_out(o):
+        return remote(
+            bound.at[0], bound.at[o], psend.at[1, o], precv.at[1, o], (ax, pitch_peer(o))
+        )
+
+    for o in range(1, npi):
+        bound_out(o).start()
+
+    for o in range(npi):
+        z = lax.rem(pz - o + npi, npi)
+        if o:
+            bound_out(o).wait_recv()
+        b_hi, b_lo = two_parts(bound[o])
+        bcat = jnp.concatenate([b_hi, b_lo], axis=1)
+        for g in range(na // span):
+            hot = place(g, z).T.astype(BF16)
+            sums = jnp.dot(hot, bcat, preferred_element_type=F32)
+            sums = sums[:, 0:nr] + sums[:, nr:2 * nr]
+            for j in range(span):
+                at = pl.multiple_of(((g * span + j) * npi + z) * cap, cap)
+                bsnd[pl.ds(at, cap), :] = sums[j * cap:(j + 1) * cap]
+
+    def block(ref, i):
+        return ref.at[pl.ds(pl.multiple_of(i * npi * cap, npi * cap), npi * cap)]
 
     def back_out(o):
-        e = lax.rem(me + o, devices)
-        return remote(block(bsnd, e), block(brcv, me), asend.at[1, o], arecv.at[1, o], dev(e))
+        return remote(
+            block(bsnd, axial_peer(o)), block(brcv, ax), asend.at[1, o], arecv.at[1, o],
+            (axial_peer(o), pz),
+        )
 
     def back_in(o):
-        e = lax.rem(me - o + devices, devices)
-        return remote(block(bsnd, e), block(brcv, e), asend.at[1, o], arecv.at[1, o], dev(e))
-
-    @pl.loop(1, devices)
-    def _(o):
+        i = lax.rem(ax - o + na, na)
+        return remote(block(bsnd, i), block(brcv, i), asend.at[1, o], arecv.at[1, o], (i, pz))
+
+    for o in range(1, na):
         back_out(o).start()
 
-    own = pl.ds(pl.multiple_of(me * cap, cap), cap)
+    own = pl.ds(pl.multiple_of(ax * npi * cap, npi * cap), npi * cap)
     brcv[own, :] = bsnd[own, :]
 
     wait_sent(first)
@@ -401,13 +445,12 @@
     wait_sent(mcopy[0])
     wait_sent(mcopy[2])
     wait_sent(mcopy[3])
-
-    @pl.loop(1, devices)
-    def _(o):
-        out_copy(o).wait_send()
-
-    @pl.loop(1, devices)
-    def _(o):
+    for o in range(1, na):
+        out_copy(o, axial_peer(o)).wait_send()
+    for o in range(1, npi):
+        part_out(o).wait_send()
+        bound_out(o).wait_send()
+    for o in range(1, na):
         back_in(o).wait_recv()
 
     @pl.loop(0, slots // 16)
@@ -419,8 +462,7 @@
     live = lax.broadcasted_iota(jnp.int32, (slots, nr), 0) < count_s[0]
     wall_out[...] = jnp.where(live, 0.5 * (wall[...] + rows[...]), wall[...])
 
-    @pl.loop(1, devices)
-    def _(o):
+    for o in range(1, na):
         back_out(o).wait_send()
 
 
@@ -481,13 +523,18 @@
             pltpu.VMEM((devices, cap + 8, nr), F32),
             pltpu.VMEM((devices * cap, nr), F32),
             pltpu.VMEM((devices * cap, nr), F32),
+            pltpu.VMEM((npi, 2 * mc, nr), F32),
+            pltpu.VMEM((npi, 2 * mc, nr), F32),
+            pltpu.VMEM((npi, 2 * mc, nr), F32),
             dma((2,)),
             dma((2, 4)),
             dma((2, 4)),
             dma((4, 4)),
             dma((4, 4)),
-            dma((2, devices)),
-            dma((2, devices)),
+            dma((2, na)),
+            dma((2, na)),
+            dma((2, npi)),
+            dma((2, npi)),
         ],
         compiler_params=pltpu.CompilerParams(
             collective_id=0, has_side_effects=True, vmem_limit_bytes=56 * 1024 * 1024

time: 139 us -> 100 us (0.72)
  Pallas kernels: 125 us -> 85.1 us
    pallas_call x1, Pallas kernels: 125 us -> 85.1 us  [on_device(): pl.pallas_call(functools.partial(kernel, na, npi, cap), out_shape=(jax.Sh...]
where the time goes in v1:
time: 100 us; the launch traced here: 98.3 us
  Pallas kernels  85.1 us (85%)
  local copies, waits for them, and re-layouts  6.31 us (6%)
  other arithmetic  5.58 us (6%)
  between operations  1.32 us (1%)
    pallas_call x1, Pallas kernels, on_device(): pl.pallas_call(functools.partial(kernel, na, npi, cap), out_shape=(jax.Sh...  85.1 us
    unnamed x7, local copies, waits for them, and re-layouts  5.47 us

profile of v1, /device:TPU:0, one launch (start us, length us, event | category | flops | bytes accessed | tf_op | source)
XLA Modules:
  0.0 98.3 jit_solution(1810972993427420549)
XLA Ops:
  1.3 1.4 %convert_reduce_fusion = s32[1024]{0:T(1024)S(1)} fusion(s32[1024]{0:T(1024)} %bitcast.12, pred[1024]{0:T(1024)(128)(4,1)S(1)} %iota_compare_fusion.2), kind=kLoop, calls=%fused_computation.2 | loop fusion | flops 6290432 | bytes 9216 | tf_op jit(solution)/shard_map/reduce_sum | solution.py:483
  2.7 1.3 %compare_select_fusion.key_v = s32[1,1024]{1,0:T(1,128)} fusion(s32[1,1024]{1,0:T(1,128)S(1)} %bitcast.14, s32[1024,1]{0,1:T(1,128)} %param.17, s32[]{:T(128)} %bitcast.9), kind=kLoop, calls=%fused_computation.5 | loop fusion | flops 4096 | bytes 12292 | tf_op jit(solution)/shard_map/jit(_where)/select_n | solution.py:484
  4.0 0.7 add_convert_fusion
  4.6 1.3 %broadcast_maximum_fusion = (s32[1024]{0:T(1024)}, s32[1024]{0:T(1024)S(1)}, s32[1024]{0:T(1024)}) fusion(s32[1024]{0:T(1024)S(1)} %convert_reduce_fusion, s32[1024]{0:T(1024)} %bitcast.13, s32[]{:T(128)} %bitcast.10, s32[1024]{0:T(1024)} %cell_s.1), kind=kLoop, calls=%fused_computation.11 | loop fusion | flops 6144 | bytes 24580 | tf_op jit(solution)/shard_map/max | solution.py:544
  6.0 0.9 select_reduce_fusion
  6.9 0.1 broadcast_in_dim.45
  7.0 0.1 broadcast_in_dim.47
  7.1 0.7 broadcast_in_dim.48.ids_v
  7.7 85.1 %window.1 = (f32[64,64,128]{2,1,0:T(8,128)}, f32[64,48,128]{2,1,0:T(8,128)}, f32[1024,128]{1,0:T(8,128)}) custom-call(s32[1024]{0:T(1024)} %cell_s.1, s32[1024]{0:T(1024)} %get-tuple-element.3.key_s, s32[1]{0:T(128)} %copy.17.count_s, s32[1,1024]{1,0:T(1,128)} %bitcast.11, s32[1,1024]{1,0:T(1,128)} %compare_select_fusion.key_v, ...), custom_call_target="tpu_custom_call" | custom-call | tf_op jit(solution)/shard_map/window/pallas_call | solution.py:495
  92.9 0.0 copy-start
  92.9 3.3 %copy.18 = f32[64,64,128]{2,1,0:T(8,128)} copy(f32[64,64,128]{2,1,0:T(8,128)} %get-tuple-element.9) | data formatting | bytes 4194304
  96.2 0.0 copy-done
  96.2 0.0 copy-start.1
  96.2 1.1 %copy.19 = f32[64,48,128]{2,1,0:T(8,128)} copy(f32[64,48,128]{2,1,0:T(8,128)S(1)} %copy-done) | data formatting | bytes 3145728
  97.3 0.3 copy-done.1
  97.6 0.8 copy.20
  (2 shorter events, 0.0 us)
Async XLA Ops:
  92.9 3.3 %copy-start = (f32[64,48,128]{2,1,0:T(8,128)S(1)}, f32[64,48,128]{2,1,0:T(8,128)}, u32[]{:S(2)}) copy-start(f32[64,48,128]{2,1,0:T(8,128)} %get-tuple-element.10) | copy-start | bytes 4718596
  96.2 1.4 %copy-start.1 = (f32[1024,128]{1,0:T(8,128)S(1)}, f32[1024,128]{1,0:T(8,128)}, u32[]{:S(2)}) copy-start(f32[1024,128]{1,0:T(8,128)} %get-tuple-element.11) | copy-start | bytes 1572868

commit v2 on v1

--- a/solution.py
+++ b/solution.py
@@ -237,21 +237,24 @@
         snd[pl.ds(i * owners, owners), 0:cap, :] = part
         snd[pl.ds(i * owners, owners), cap:cap + 8, :] = ids_v[pl.ds(i * owners, owners)]
 
-    def out_copy(o, j):
+    def out_copy(o, zo):
+        i, z = axial_peer(o), pitch_peer(zo)
         return remote(
-            snd.at[pl.ds(j * npi, npi)], rcv.at[pl.ds(ax * npi, npi)], asend.at[0, o], arecv.at[0, o],
-            (axial_peer(o), pz),
-        )
-
-    def in_copy(o):
-        i = lax.rem(ax - o + na, na)
+            snd.at[i * npi + z], rcv.at[ax * npi + z], asend.at[0, zo, o], arecv.at[0, zo, o], (i, pz)
+        )
+
+    def in_copy(o, zo):
+        i, z = lax.rem(ax - o + na, na), pitch_peer(zo)
         return remote(
-            snd.at[pl.ds(i * npi, npi)], rcv.at[pl.ds(i * npi, npi)], asend.at[0, o], arecv.at[0, o],
-            (i, pz),
-        )
-
-    for o in range(1, na):
-        out_copy(o, axial_peer(o)).start()
+            snd.at[i * npi + z], rcv.at[i * npi + z], asend.at[0, zo, o], arecv.at[0, zo, o], (i, pz)
+        )
+
+    z_order = tuple(range(1, npi)) + (0,)
+    for zo in z_order:
+
+        @pl.loop(1, na)
+        def _(o, zo=zo):
+            out_copy(o, zo).start()
 
     rcv[pl.ds(ax * npi, npi)] = snd[pl.ds(ax * npi, npi)]
 
@@ -301,8 +304,10 @@
         temp, change = rate(spad, 1, a)
         fluid_out[a] = avg[pl.ds(pl.multiple_of(a * cp, cp), cp), :] + 0.5 * change
 
-    for o in range(1, na):
-        in_copy(o).wait_recv()
+    def got_rows(zo):
+        @pl.loop(1, na)
+        def _(o):
+            in_copy(o, zo).wait_recv()
 
     lane_p = lax.broadcasted_iota(jnp.int32, (8, nr), 1)
     row_p = lax.broadcasted_iota(jnp.int32, (2 * mc, nr), 0).astype(F32) + 1.0
@@ -340,8 +345,10 @@
         )
 
     for o in range(1, npi):
+        got_rows(o)
         part_snd[o] = injected(pitch_peer(o))
         part_out(o).start()
+    got_rows(0)
     mine = injected(pz)
     for o in range(1, npi):
         part_out(o).wait_recv()
@@ -407,11 +414,28 @@
     for o in range(1, npi):
         bound_out(o).start()
 
-    for o in range(npi):
-        z = lax.rem(pz - o + npi, npi)
-        if o:
-            bound_out(o).wait_recv()
-        b_hi, b_lo = two_parts(bound[o])
+    def block(ref, e):
+        return ref.at[pl.ds(pl.multiple_of(e * cap, cap), cap)]
+
+    def back_out(o, zo):
+        i, z = axial_peer(o), lax.rem(pz - zo + npi, npi)
+        return remote(
+            block(bsnd, i * npi + z), block(brcv, ax * npi + z), asend.at[1, zo, o], arecv.at[1, zo, o],
+            (i, pz),
+        )
+
+    def back_in(o, zo):
+        i, z = lax.rem(ax - o + na, na), lax.rem(pz - zo + npi, npi)
+        return remote(
+            block(bsnd, i * npi + z), block(brcv, i * npi + z), asend.at[1, zo, o], arecv.at[1, zo, o],
+            (i, pz),
+        )
+
+    for zo in range(npi):
+        z = lax.rem(pz - zo + npi, npi)
+        if zo:
+            bound_out(zo).wait_recv()
+        b_hi, b_lo = two_parts(bound[zo])
         bcat = jnp.concatenate([b_hi, b_lo], axis=1)
         for g in range(na // span):
             hot = place(g, z).T.astype(BF16)
@@ -421,21 +445,9 @@
                 at = pl.multiple_of(((g * span + j) * npi + z) * cap, cap)
                 bsnd[pl.ds(at, cap), :] = sums[j * cap:(j + 1) * cap]
 
-    def block(ref, i):
-        return ref.at[pl.ds(pl.multiple_of(i * npi * cap, npi * cap), npi * cap)]
-
-    def back_out(o):
-        return remote(
-            block(bsnd, axial_peer(o)), block(brcv, ax), asend.at[1, o], arecv.at[1, o],
-            (axial_peer(o), pz),
-        )
-
-    def back_in(o):
-        i = lax.rem(ax - o + na, na)
-        return remote(block(bsnd, i), block(brcv, i), asend.at[1, o], arecv.at[1, o], (i, pz))
-
-    for o in range(1, na):
-        back_out(o).start()
+        @pl.loop(1, na)
+        def _(o, zo=zo):
+            back_out(o, zo).start()
 
     own = pl.ds(pl.multiple_of(ax * npi * cap, npi * cap), npi * cap)
     brcv[own, :] = bsnd[own, :]
@@ -445,13 +457,20 @@
     wait_sent(mcopy[0])
     wait_sent(mcopy[2])
     wait_sent(mcopy[3])
-    for o in range(1, na):
-        out_copy(o, axial_peer(o)).wait_send()
+    for zo in range(npi):
+
+        @pl.loop(1, na)
+        def _(o, zo=zo):
+            out_copy(o, zo).wait_send()
+
     for o in range(1, npi):
         part_out(o).wait_send()
         bound_out(o).wait_send()
-    for o in range(1, na):
-        back_in(o).wait_recv()
+    for zo in range(npi):
+
+        @pl.loop(1, na)
+        def _(o, zo=zo):
+            back_in(o, zo).wait_recv()
 
     @pl.loop(0, slots // 16)
     def _(i):
@@ -462,8 +481,11 @@
     live = lax.broadcasted_iota(jnp.int32, (slots, nr), 0) < count_s[0]
     wall_out[...] = jnp.where(live, 0.5 * (wall[...] + rows[...]), wall[...])
 
-    for o in range(1, na):
-        back_out(o).wait_send()
+    for zo in range(npi):
+
+        @pl.loop(1, na)
+        def _(o, zo=zo):
+            back_out(o, zo).wait_send()
 
 
 def on_device(
@@ -531,8 +553,8 @@
             dma((2, 4)),
             dma((4, 4)),
             dma((4, 4)),
-            dma((2, na)),
-            dma((2, na)),
+            dma((2, npi, na)),
+            dma((2, npi, na)),
             dma((2, npi)),
             dma((2, npi)),
         ],

time: 100 us -> 91.3 us (0.913); the launches traced: 98.3 us -> 90.9 us
  Pallas kernels: 85.1 us -> 77.7 us
    pallas_call x1, Pallas kernels: 85.1 us -> 77.7 us  [on_device(): pl.pallas_call(functools.partial(kernel, na, npi, cap), out_shape=(jax.Sh...]
where the time goes in v2:
time: 91.3 us; the launch traced here: 90.9 us
  Pallas kernels  77.7 us (85%)
  local copies, waits for them, and re-layouts  6.31 us (7%)
  other arithmetic  5.58 us (6%)
  between operations  1.32 us (1%)
    pallas_call x1, Pallas kernels, on_device(): pl.pallas_call(functools.partial(kernel, na, npi, cap), out_shape=(jax.Sh...  77.7 us
    unnamed x7, local copies, waits for them, and re-layouts  5.47 us

profile of v2, /device:TPU:0, one launch (start us, length us, event | category | flops | bytes accessed | tf_op | source)
XLA Modules:
  0.0 90.9 jit_solution(9496406191244656709)
XLA Ops:
  1.3 1.4 %convert_reduce_fusion = s32[1024]{0:T(1024)S(1)} fusion(s32[1024]{0:T(1024)} %bitcast.12, pred[1024]{0:T(1024)(128)(4,1)S(1)} %iota_compare_fusion.2), kind=kLoop, calls=%fused_computation.2 | loop fusion | flops 6290432 | bytes 9216 | tf_op jit(solution)/shard_map/reduce_sum | solution.py:505
  2.7 1.3 %compare_select_fusion.key_v = s32[1,1024]{1,0:T(1,128)} fusion(s32[1,1024]{1,0:T(1,128)S(1)} %bitcast.14, s32[1024,1]{0,1:T(1,128)} %param.17, s32[]{:T(128)} %bitcast.9), kind=kLoop, calls=%fused_computation.5 | loop fusion | flops 4096 | bytes 12292 | tf_op jit(solution)/shard_map/jit(_where)/select_n | solution.py:506
  4.0 0.7 add_convert_fusion
  4.6 1.3 %broadcast_maximum_fusion = (s32[1024]{0:T(1024)}, s32[1024]{0:T(1024)S(1)}, s32[1024]{0:T(1024)}) fusion(s32[1024]{0:T(1024)S(1)} %convert_reduce_fusion, s32[1024]{0:T(1024)} %bitcast.13, s32[]{:T(128)} %bitcast.10, s32[1024]{0:T(1024)} %cell_s.1), kind=kLoop, calls=%fused_computation.11 | loop fusion | flops 6144 | bytes 24580 | tf_op jit(solution)/shard_map/max | solution.py:566
  6.0 0.9 %select_reduce_fusion = f32[2048]{0:T(1024)S(1)} fusion(f32[1024]{0:T(1024)S(1)} %add_convert_fusion, s32[1024]{0:T(1024)S(1)} %get-tuple-element.4), kind=kLoop, calls=%fused_computation | loop fusion | flops 6289408 | bytes 16384 | tf_op jit(solution)/shard_map/reduce_sum | solution.py:508
  6.9 0.1 broadcast_in_dim.45
  7.0 0.1 broadcast_in_dim.47
  7.1 0.7 broadcast_in_dim.48.ids_v
  7.7 77.7 %window.1 = (f32[64,64,128]{2,1,0:T(8,128)}, f32[64,48,128]{2,1,0:T(8,128)}, f32[1024,128]{1,0:T(8,128)}) custom-call(s32[1024]{0:T(1024)} %cell_s.1, s32[1024]{0:T(1024)} %get-tuple-element.3.key_s, s32[1]{0:T(128)} %copy.17.count_s, s32[1,1024]{1,0:T(1,128)} %bitcast.11, s32[1,1024]{1,0:T(1,128)} %compare_select_fusion.key_v, ...), custom_call_target="tpu_custom_call" | custom-call | tf_op jit(solution)/shard_map/window/pallas_call | solution.py:517
  85.4 0.0 copy-start
  85.4 3.3 %copy.18 = f32[64,64,128]{2,1,0:T(8,128)} copy(f32[64,64,128]{2,1,0:T(8,128)} %get-tuple-element.9) | data formatting | bytes 4194304
  88.7 0.0 copy-done
  88.7 0.0 copy-start.1
  88.7 1.1 %copy.19 = f32[64,48,128]{2,1,0:T(8,128)} copy(f32[64,48,128]{2,1,0:T(8,128)S(1)} %copy-done) | data formatting | bytes 3145728
  89.9 0.3 copy-done.1
  90.1 0.8 copy.20
  (2 shorter events, 0.0 us)
Async XLA Ops:
  85.4 3.3 %copy-start = (f32[64,48,128]{2,1,0:T(8,128)S(1)}, f32[64,48,128]{2,1,0:T(8,128)}, u32[]{:S(2)}) copy-start(f32[64,48,128]{2,1,0:T(8,128)} %get-tuple-element.10) | copy-start | bytes 4718596
  88.7 1.4 %copy-start.1 = (f32[1024,128]{1,0:T(8,128)S(1)}, f32[1024,128]{1,0:T(8,128)}, u32[]{:S(2)}) copy-start(f32[1024,128]{1,0:T(8,128)} %get-tuple-element.11) | copy-start | bytes 1572868
